TPU v7x, 32 devices: a whole 2x2x4 slice. The times are simulated.
32 devices in a mesh: slides: 2 (over y), tile: 4 (over z), col: 2 (over x), mp: 2 (over core).
Axes of the slice: x: 2, y: 2, z: 4, core: 2. Of those that a mesh axis runs over, the one named last changes fastest.
Arguments:
- patches: bfloat16 [128, 48, 1024], P(('slides', 'tile'), 'col', 'mp'), parts along dimension 0, may hold values from -8 to 8
- tissue: int32 [128, 48], P(('slides', 'tile'), 'col'), parts along dimension 0, may hold values from 0 to 1, as said below
- conv_weight: bfloat16 [3, 3, 1024], P(None, None, 'mp'), may hold values from -2 to 2
- ln_gain: float32 [1024], P('mp'), may hold values from 0.1 to 1.9
- qkv_weight: bfloat16 [3, 1024, 1024], P(None, None, 'mp'), may hold values from -0.1875 to 0.1875
- omega: float32 [256, 64], replicated, may hold values from -6 to 6
- out_weight: bfloat16 [1024, 1024], P('mp'), may hold values from -0.1875 to 0.1875
Outputs:
- layer_out: bfloat16 [128, 48, 1024], P(('slides', 'tile'), 'col', 'mp'), parts along dimension 0
There are 2 independent parts, one for each index of `slides`. A program takes and returns all parts, laid end to end along the dimension named above; an argument that names none is the same for every part. Nothing has to cross between parts.
Inputs may be any that keep to these rules, and one draw needn't show every extreme that they name: 1 marks tissue, 0 background; the slide's first patch is tissue.
All inputs are finite; a program needn't handle non-finite values.
Results may differ from a plain program's by a relative error of at most 0.0065.
Values may be sent and summed in bfloat16 or wider, within the bound.
A program may use at most 64 MiB of HBM per device.

v0:
```python
import math

import jax
import jax.numpy as jnp
from jax import lax
from jax.sharding import PartitionSpec as P

E = 64
M = 256


def extended(cells, sides, width):
    for axis, dim in sides:
        count = lax.axis_size(axis)
        ends = count - 1
        head = lax.slice_in_dim(cells, 0, width, axis=dim)
        tail = lax.slice_in_dim(cells, cells.shape[dim] - width, cells.shape[dim], axis=dim)
        cells = jnp.concatenate(
            [
                lax.ppermute(tail, axis, [(i, (i + 1) % count) for i in range(ends)]),
                cells,
                lax.ppermute(head, axis, [((i + 1) % count, i) for i in range(ends)]),
            ],
            axis=dim,
        )
    return cells


def features(scaled, omega):
    lifted = jnp.einsum("the,me->thm", scaled, omega, precision=lax.Precision.HIGHEST)
    square = 0.5 * jnp.sum(scaled * scaled, axis=-1, keepdims=True)
    return (jnp.exp(lifted - square) / math.sqrt(M)).astype(jnp.bfloat16)


def split_pair(values):
    upper = values.astype(jnp.bfloat16)
    lower = (values - upper.astype(jnp.float32)).astype(jnp.bfloat16)
    return (upper, lower)


def shards(patches, tissue, conv_weight, ln_gain, qkv_weight, omega, out_weight):
    rows_here, cols_here, half = patches.shape
    tokens = rows_here * cols_here
    padded = extended(patches, (("tile", 0), ("col", 1)), 1)
    widened = padded.astype(jnp.float32)
    kernel = conv_weight.astype(jnp.float32)
    stem = patches.astype(jnp.float32)
    for row_off in range(3):
        for col_off in range(3):
            stem = (
                stem
                + kernel[row_off, col_off]
                * widened[row_off : row_off + rows_here, col_off : col_off + cols_here]
            )
    flat = stem.reshape(tokens, half)
    totals = lax.psum((jnp.sum(flat, axis=1), jnp.sum(flat * flat, axis=1)), "mp")
    width = half * lax.axis_size("mp")
    mean_val = totals[0] / width
    var_val = totals[1] / width - mean_val * mean_val
    normed = ((flat - mean_val[:, None]) * lax.rsqrt(var_val + 1e-05)[:, None] * ln_gain).astype(
        jnp.bfloat16
    )
    projected = jnp.einsum(
        "td,cdf->ctf",
        lax.all_gather(normed, "mp", axis=1, tiled=True),
        qkv_weight,
        preferred_element_type=jnp.float32,
    ).astype(jnp.bfloat16)
    heads_here = qkv_weight.shape[2] // E
    scale = E ** (-0.25)
    key_part = projected[1].astype(jnp.float32).reshape(tokens, heads_here, E) * scale
    keep = tissue.reshape(tokens).astype(jnp.bfloat16)
    key_feat = features(key_part, omega) * keep[:, None, None]
    value_part = projected[2].reshape(tokens, heads_here, E)
    state = jnp.einsum("the,thm->hem", value_part, key_feat, preferred_element_type=jnp.float32)
    key_sum = jnp.sum(key_feat.astype(jnp.float32), axis=0)
    kv_state, normalizer = lax.psum((state, key_sum), ("tile", "col"))
    query_part = projected[0].astype(jnp.float32).reshape(tokens, heads_here, E) * scale
    query_feat = features(query_part, omega)
    state_upper, state_lower = split_pair(kv_state)
    norm_upper, norm_lower = split_pair(normalizer)
    numer = jnp.einsum("thm,hem->the", query_feat, state_upper, preferred_element_type=jnp.float32)
    numer = numer + jnp.einsum(
        "thm,hem->the", query_feat, state_lower, preferred_element_type=jnp.float32
    )
    denom = jnp.einsum("thm,hm->th", query_feat, norm_upper, preferred_element_type=jnp.float32)
    denom = denom + jnp.einsum(
        "thm,hm->th", query_feat, norm_lower, preferred_element_type=jnp.float32
    )
    attended = (numer / denom[:, :, None]).astype(jnp.bfloat16).reshape(tokens, heads_here * E)
    mixed = (
        lax.psum_scatter(
            lax.dot_general(
                out_weight, attended, (((0,), (1,)), ((), ())), preferred_element_type=jnp.float32
            ).astype(jnp.bfloat16),
            "mp",
            scatter_dimension=0,
            tiled=True,
        )
        .astype(jnp.float32)
        .T
    )
    return (flat + mixed).astype(jnp.bfloat16).reshape(rows_here, cols_here, half)


def solution(mesh):
    placed = (
        P(("slides", "tile"), "col", "mp"),
        P(("slides", "tile"), "col"),
        P(None, None, "mp"),
        P("mp"),
        P(None, None, "mp"),
        P(),
        P("mp", None),
    )
    return jax.shard_map(
        shards,
        mesh=mesh,
        in_specs=placed,
        out_specs=P(("slides", "tile"), "col", "mp"),
        check_vma=False,
    )
```

profile of v0, /device:TPU:29, one launch (start us, length us, event | category | flops | bytes accessed | tf_op | source)
XLA Modules:
  0.0 166.2 jit_solution(4556089762340972274)
XLA Ops:
  6.5 0.9 fusion.34
  7.5 1.4 collective-permute-start
  8.9 4.0 %collective-permute-start.1 = (bf16[1,24,512]{2,1,0:T(8,128)(2,1)S(1)}, bf16[1,24,512]{2,1,0:T(8,128)(2,1)S(1)}, u32[]{:S(2)}, u32[]{:S(2)}) collective-permute-start(bf16[1,24,512]{2,1,0:T(8,128)(2,1)S(1)} %get-tuple-element.14), channel_id=1, source_target_pairs={{4,0},{8,4},{12,8},{5,1},{9,5},{13,9},{6,2},{10,6},{14,10},{7,3},{... | collective-permute-start | bytes 73736 | tf_op jit(solution)/shard_map/ppermute | solution.py:22
  12.9 1.0 constant_dynamic-update-slice_fusion.1
  14.0 0.7 copy-done.4
  15.4 3.7 %collective-permute-start.2 = (bf16[18,1,512]{2,1,0:T(2,128)(2,1)}, bf16[18,1,512]{2,1,0:T(2,128)(2,1)}, u32[]{:S(2)}, u32[]{:S(2)}) collective-permute-start(bf16[18,1,512]{2,1,0:T(2,128)(2,1)} %get-tuple-element.12), channel_id=1, source_target_pairs={{0,2},{1,3},{4,6},{5,7},{8,10},{9,11},{12,14},{13,15},{16,18},{17,... | collective-permute-start | bytes 55304 | tf_op jit(solution)/shard_map/ppermute | solution.py:20
  19.1 1.3 collective-permute-start.3
  20.4 1.5 fusion.35
  21.9 0.7 convert_element_type.94
  23.3 0.8 collective-permute-done.3
  24.1 1.2 maximum_convert_fusion
  25.5 1.7 %fusion.31 = (f32[16,24]{1,0:T(8,128)S(1)}, f32[16,24]{1,0:T(8,128)S(1)}, f32[16,24,512]{2,1,0:T(8,128)}) fusion(f32[18,26,512]{2,1,0:T(8,128)S(1)} %maximum_convert_fusion, f32[512]{0:T(512)S(1)} %bitcast.83, f32[512]{0:T(512)S(1)} %bitcast.82, f32[512]{0:T(512)S(1)} %bitcast.81, f32[512]{0:T(512)S(1)} %bitcast.80, f32[512]{0:T(512)S(1)} %bitcast.79, ...), kind=kLoop, calls=%fused_computation.65 | loop fusion | flops 4324608 | bytes 8279040 | tf_op jit(solution)/shard_map/reduce_sum | solution.py:56
  27.4 5.2 %all-reduce = (f32[384]{0:T(512)S(1)}, f32[384]{0:T(512)S(1)}) all-reduce(f32[384]{0:T(512)S(1)} %reduce_sum.52, f32[384]{0:T(512)S(1)} %reduce_sum.50), channel_id=1, replica_groups=mesh['slides'=2,'tile'=4,'col'=2,'mp'=2] {'mp'}, use_global_device_ids=true, to_apply=%region_3.0 | all-reduce | flops 768 | bytes 6144 | tf_op jit(solution)/shard_map/psum | solution.py:56
  32.6 1.3 fusion.19
  33.9 2.4 %all_gather.3 = bf16[384,1024]{1,0:T(8,128)(2,1)S(1)} all-gather(bf16[384,512]{1,0:T(8,128)(2,1)S(1)} %fusion.19), channel_id=1, replica_groups=mesh['slides'=2,'tile'=4,'col'=2,'mp'=2] {'mp'}, dimensions={1}, use_global_device_ids=true | all-gather | bytes 1179648 | tf_op jit(solution)/shard_map/all_gather | solution.py:65
  36.3 1.4 fusion.1
  37.7 0.8 slice.120
  38.5 1.4 convert_multiply_fusion.1
  39.8 1.2 copy.11
  41.1 2.3 %copy.12 = f32[1,384,512]{1,2,0:T(8,128)} copy(f32[1,384,512]{2,1,0:T(8,128)} %get-tuple-element.10) | data formatting | bytes 1572864 | tf_op jit(solution)/shard_map/mul | solution.py:71
  43.3 1.2 multiply_reduce_fusion.1
  44.6 5.8 %convert_reduce_fusion = (f32[8,256]{1,0:T(8,128)S(1)}, bf16[384,8,256]{2,0,1:T(8,128)(2,1)}) fusion(bf16[384]{0:T(512)(128)(2,1)S(1)} %copy-done.15, f32[384,8]{0,1:T(8,128)S(1)} %broadcast_multiply_fusion.1, f32[384,8,64]{0,2,1:T(8,128)} %bitcast.71, f32[256,64]{0,1:T(8,128)} %param.12), kind=kOutput, calls=%fused_computation | convolution fusion | flops 608696320 | bytes 2446080 | tf_op jit(solution)/shard_map/the,me->thm/dot_general | solution.py:30
  50.3 13.1 %psum.31 = f32[8,256]{1,0:T(8,128)S(1)} all-reduce(f32[8,256]{1,0:T(8,128)S(1)} %get-tuple-element.29), channel_id=1, replica_groups=mesh['slides'=2,'tile'=4,'col'=2,'mp'=2] {'tile','col'}, use_global_device_ids=true, to_apply=%region_8.0 | all-reduce | flops 2048 | bytes 16384 | tf_op jit(solution)/shard_map/psum | solution.py:77
  63.4 2.6 %fusion.36 = f32[8,64,256]{2,1,0:T(8,128)} fusion(bf16[384,8,64]{0,2,1:T(8,128)(2,1)S(1)} %bitcast.74, bf16[384,8,256]{2,0,1:T(8,128)(2,1)} %get-tuple-element.30), kind=kOutput, calls=%fused_computation.69 | convolution fusion | flops 100663296 | bytes 2490368 | tf_op jit(solution)/shard_map/the,thm->hem/dot_general | solution.py:75
  66.3 2.3 %copy.13 = f32[1,384,512]{1,2,0:T(8,128)} copy(f32[1,384,512]{2,1,0:T(8,128)} %get-tuple-element.11) | data formatting | bytes 1572864 | tf_op jit(solution)/shard_map/mul | solution.py:78
  68.6 1.2 multiply_reduce_fusion
  69.8 4.4 %multiply_convert_fusion = bf16[384,8,256]{2,0,1:T(8,128)(2,1)S(1)} fusion(f32[384,8,64]{0,2,1:T(8,128)} %bitcast.73, f32[384,8]{0,1:T(8,128)S(1)} %broadcast_multiply_fusion, f32[256,64]{0,1:T(8,128)S(1)} %copy-done.17), kind=kOutput, calls=%fused_computation.1 | convolution fusion | flops 606339072 | bytes 2437120 | tf_op jit(solution)/shard_map/the,me->thm/dot_general | solution.py:30
  75.3 65.6 %all-reduce.3.cloned.1.call-done = f32[8,64,256]{2,1,0:T(8,128)} async-done(((f32[8,64,256]{2,1,0:T(8,128)}), f32[8,64,256]{2,1,0:T(8,128)}) %all-reduce.3.cloned.1.call-update) | async-done | bytes 524304 | tf_op jit(solution)/shard_map/psum | solution.py:77
  141.0 2.3 %fusion.21 = f32[8,64,384]{2,1,0:T(8,128)S(1)} fusion(bf16[384,8,256]{2,0,1:T(8,128)(2,1)} %copy-done.1, f32[8,64,256]{2,1,0:T(8,128)} %all-reduce.3.cloned.1.call-done), kind=kOutput, calls=%fused_computation.45 | convolution fusion | flops 100794368 | bytes 2883584 | tf_op jit(solution)/shard_map/thm,hem->the/dot_general | solution.py:82
  144.5 1.5 fusion.2
  146.0 11.3 %reduce-scatter.2.cloned.1.call-done = bf16[512,384]{0,1:T(8,128)(2,1)} async-done(((bf16[1024,384]{0,1:T(8,128)(2,1)}), bf16[512,384]{0,1:T(8,128)(2,1)}) %reduce-scatter.2.cloned.1.call-update) | async-done | bytes 393232 | tf_op jit(solution)/shard_map/reduce_scatter | solution.py:92
  157.3 2.1 %fusion.15 = bf16[384,512]{1,0:T(8,128)(2,1)} fusion(f32[16,24,512]{2,1,0:T(8,128)} %get-tuple-element.9, bf16[512,384]{0,1:T(8,128)(2,1)} %reduce-scatter.2.cloned.1.call-done), kind=kLoop, calls=%fused_computation.31 | loop fusion | flops 589824 | bytes 1572864 | tf_op jit(solution)/shard_map/convert_element_type | solution.py:103
  (56 shorter events, 4.2 us)
Async XLA Ops:
  6.5 29.8 %copy-start = (bf16[3,1024,512]{2,1,0:T(8,128)(2,1)S(1)}, bf16[3,1024,512]{2,1,0:T(8,128)(2,1)}, u32[]{:S(2)}) copy-start(bf16[3,1024,512]{2,1,0:T(8,128)(2,1)} %param.11) | copy-start | bytes 9437188
  6.5 18.8 %copy-start.3 = (bf16[16,24,512]{2,1,0:T(8,128)(2,1)S(1)}, bf16[16,24,512]{2,1,0:T(8,128)(2,1)}, u32[]{:S(2)}) copy-start(bf16[16,24,512]{2,1,0:T(8,128)(2,1)} %param.7) | copy-start | bytes 1179652
  6.5 134.4 %all-reduce.3.cloned.1.call-start = ((), (), s32[]{:S(2)}) async-start(), calls=%async_computation.1 | async-start | bytes 1048576 | tf_op jit(solution)/shard_map/psum | solution.py:77
  7.5 5.4 %collective-permute-start = (bf16[1,24,512]{2,1,0:T(8,128)(2,1)S(1)}, bf16[1,24,512]{2,1,0:T(8,128)(2,1)S(1)}, u32[]{:S(2)}, u32[]{:S(2)}) collective-permute-start(bf16[1,24,512]{2,1,0:T(8,128)(2,1)S(1)} %get-tuple-element.15), channel_id=1, source_target_pairs={{0,4},{4,8},{8,12},{1,5},{5,9},{9,13},{2,6},{6,10},{10,14},{3,7},{... | collective-permute-start | bytes 73736 | tf_op jit(solution)/shard_map/ppermute | solution.py:20
  8.9 5.0 %collective-permute-start.1 = (bf16[1,24,512]{2,1,0:T(8,128)(2,1)S(1)}, bf16[1,24,512]{2,1,0:T(8,128)(2,1)S(1)}, u32[]{:S(2)}, u32[]{:S(2)}) collective-permute-start(bf16[1,24,512]{2,1,0:T(8,128)(2,1)S(1)} %get-tuple-element.14), channel_id=1, source_target_pairs={{4,0},{8,4},{12,8},{5,1},{9,5},{13,9},{6,2},{10,6},{14,10},{7,3},{... | collective-permute-start | bytes 73736 | tf_op jit(solution)/shard_map/ppermute | solution.py:22
  13.9 0.8 copy-start.4
  15.4 7.9 %collective-permute-start.2 = (bf16[18,1,512]{2,1,0:T(2,128)(2,1)}, bf16[18,1,512]{2,1,0:T(2,128)(2,1)}, u32[]{:S(2)}, u32[]{:S(2)}) collective-permute-start(bf16[18,1,512]{2,1,0:T(2,128)(2,1)} %get-tuple-element.12), channel_id=1, source_target_pairs={{0,2},{1,3},{4,6},{5,7},{8,10},{9,11},{12,14},{13,15},{16,18},{17,... | collective-permute-start | bytes 55304 | tf_op jit(solution)/shard_map/ppermute | solution.py:20
  19.1 5.0 %collective-permute-start.3 = (bf16[18,1,512]{2,1,0:T(2,128)(2,1)}, bf16[18,1,512]{2,1,0:T(2,128)(2,1)}, u32[]{:S(2)}, u32[]{:S(2)}) collective-permute-start(bf16[18,1,512]{2,1,0:T(2,128)(2,1)} %get-tuple-element.13), channel_id=1, source_target_pairs={{2,0},{3,1},{6,4},{7,5},{10,8},{11,9},{14,12},{15,13},{18,16},{19,... | collective-permute-start | bytes 55304 | tf_op jit(solution)/shard_map/ppermute | solution.py:22
  23.2 2.2 %copy-start.6 = (f32[1,1,512]{2,1,0:T(1,128)S(1)}, f32[1,1,512]{2,1,0:T(1,128)}, u32[]{:S(2)}) copy-start(f32[1,1,512]{2,1,0:T(1,128)} %get-tuple-element.16) | copy-start | bytes 6148
  23.2 2.2 %copy-start.7 = (f32[1,1,512]{2,1,0:T(1,128)S(1)}, f32[1,1,512]{2,1,0:T(1,128)}, u32[]{:S(2)}) copy-start(f32[1,1,512]{2,1,0:T(1,128)} %get-tuple-element.17) | copy-start | bytes 6148
  23.2 2.2 %copy-start.8 = (f32[1,1,512]{2,1,0:T(1,128)S(1)}, f32[1,1,512]{2,1,0:T(1,128)}, u32[]{:S(2)}) copy-start(f32[1,1,512]{2,1,0:T(1,128)} %get-tuple-element.18) | copy-start | bytes 6148
  23.2 2.2 %copy-start.9 = (f32[1,1,512]{2,1,0:T(1,128)S(1)}, f32[1,1,512]{2,1,0:T(1,128)}, u32[]{:S(2)}) copy-start(f32[1,1,512]{2,1,0:T(1,128)} %get-tuple-element.19) | copy-start | bytes 6148
  23.2 2.2 %copy-start.10 = (f32[1,1,512]{2,1,0:T(1,128)S(1)}, f32[1,1,512]{2,1,0:T(1,128)}, u32[]{:S(2)}) copy-start(f32[1,1,512]{2,1,0:T(1,128)} %get-tuple-element.20) | copy-start | bytes 6148
  23.2 2.2 %copy-start.11 = (f32[1,1,512]{2,1,0:T(1,128)S(1)}, f32[1,1,512]{2,1,0:T(1,128)}, u32[]{:S(2)}) copy-start(f32[1,1,512]{2,1,0:T(1,128)} %get-tuple-element.21) | copy-start | bytes 6148
  23.2 2.2 %copy-start.12 = (f32[1,1,512]{2,1,0:T(1,128)S(1)}, f32[1,1,512]{2,1,0:T(1,128)}, u32[]{:S(2)}) copy-start(f32[1,1,512]{2,1,0:T(1,128)} %get-tuple-element.22) | copy-start | bytes 6148
  23.3 2.2 %copy-start.13 = (f32[1,1,512]{2,1,0:T(1,128)S(1)}, f32[1,1,512]{2,1,0:T(1,128)}, u32[]{:S(2)}) copy-start(f32[1,1,512]{2,1,0:T(1,128)} %get-tuple-element.23) | copy-start | bytes 6148
  23.3 2.2 %copy-start.14 = (f32[1,1,512]{2,1,0:T(1,128)S(1)}, f32[1,1,512]{2,1,0:T(1,128)}, u32[]{:S(2)}) copy-start(f32[1,1,512]{2,1,0:T(1,128)} %get-tuple-element.24) | copy-start | bytes 6148
  39.8 4.7 %copy-start.15 = (bf16[384]{0:T(512)(128)(2,1)S(1)}, bf16[384]{0:T(512)(128)(2,1)}, u32[]{:S(2)}) copy-start(bf16[384]{0:T(512)(128)(2,1)} %convert_element_type.95) | copy-start | bytes 2308
  66.0 3.8 %copy-start.17 = (f32[256,64]{0,1:T(8,128)S(1)}, f32[256,64]{0,1:T(8,128)}, u32[]{:S(2)}) copy-start(f32[256,64]{0,1:T(8,128)} %param.12) | copy-start | bytes 196612
  66.1 91.2 %reduce-scatter.2.cloned.1.call-start = ((), (), s32[]{:S(2)}) async-start(), calls=%async_computation.2 | async-start | bytes 1179648 | tf_op jit(solution)/shard_map/reduce_scatter | solution.py:92
  74.2 1.2 copy-start.1
  141.0 2.3 %copy-start.2 = (bf16[384,8,256]{2,0,1:T(8,128)(2,1)S(1)}, bf16[384,8,256]{2,0,1:T(8,128)(2,1)}, u32[]{:S(2)}) copy-start(bf16[384,8,256]{2,0,1:T(8,128)(2,1)} %copy-done.1) | copy-start | bytes 4718596
  141.0 2.3 %copy-start.5 = (f32[8,64,256]{2,1,0:T(8,128)S(1)}, f32[8,64,256]{2,1,0:T(8,128)}, u32[]{:S(2)}) copy-start(f32[8,64,256]{2,1,0:T(8,128)} %all-reduce.3.cloned.1.call-done) | copy-start | bytes 1572868
  143.3 1.2 copy-start.16
Sparse Core Ops, SparseCore 0:
  66.2 74.7 all-reduce.2
  146.1 11.1 reduce-scatter.1
where the time goes:
time: 168 us; the launch traced here: 166 us
  waiting for transfers between devices  77.8 us (46%)
  blocking collectives  20.7 us (12%)
  matrix products  19.5 us (12%)
  between operations  13.8 us (8%)
  local copies, waits for them, and re-layouts  13 us (8%)
  other arithmetic  10.9 us (6%)
  starting transfers between devices  10.6 us (6%)
    psum x1, waiting for transfers between devices, shards(): kv_state, normalizer = lax.psum((state, key_sum), ('tile', 'col'))  65.6 us
    psum x1, blocking collectives, shards(): kv_state, normalizer = lax.psum((state, key_sum), ('tile', 'col'))  13.1 us
    reduce_scatter x1, waiting for transfers between devices, shards(): lax.psum_scatter(lax.dot_general(out_weight, attended, (((0,), (1,)), (()...  11.3 us
    dot_general x2, matrix products, features(): jnp.einsum('the,me->thm', scaled, omega, precision=lax.Precision.HIGHEST)  10.1 us
    ppermute x2, starting transfers between devices, extended(): lax.ppermute(head, axis, [((i + 1) % count, i) for i in range(ends)])  5.27 us
    psum x1, blocking collectives, shards(): lax.psum((jnp.sum(flat, axis=1), jnp.sum(flat * flat, axis=1)), 'mp')  5.22 us
    ppermute x2, starting transfers between devices, extended(): lax.ppermute(tail, axis, [(i, (i + 1) % count) for i in range(ends)])  5.13 us
  transfers between devices with their start and end apart: 6, of which 3 were waited for; matrix products, arithmetic and copies ran while one was open for 8% of the time, Pallas kernels for 0%

commit v1 on v0

--- a/solution.py
+++ b/solution.py
@@ -1,8 +1,11 @@
+import functools
 import math
 
 import jax
 import jax.numpy as jnp
 from jax import lax
+from jax.experimental import pallas as pl
+from jax.experimental.pallas import tpu as pltpu
 from jax.sharding import PartitionSpec as P
 
 E = 64
@@ -103,7 +106,473 @@
     return (flat + mixed).astype(jnp.bfloat16).reshape(rows_here, cols_here, half)
 
 
+MESH = pl.DeviceIdType.MESH
+F32 = jnp.float32
+BF16 = jnp.bfloat16
+
+
+def remote(src, dst, send, recv, **where):
+    return pltpu.make_async_remote_copy(
+        src_ref=src, dst_ref=dst, send_sem=send, recv_sem=recv, device_id=where, device_id_type=MESH
+    )
+
+
+def layer_kernel(
+    tiles,
+    patches_ref,
+    tissue_ref,
+    conv_ref,
+    gain_ref,
+    qkv_ref,
+    omega_ref,
+    outw_ref,
+    out_ref,
+    pbuf,
+    padded,
+    rowh,
+    colh,
+    edge,
+    small,
+    qkvw,
+    wout,
+    stem,
+    nrm,
+    keep,
+    lift,
+    kbuf,
+    vbuf,
+    qbuf,
+    qfb,
+    rs_send,
+    rs_recv,
+    ag,
+    rd,
+    att,
+    load_sem,
+    patch_sem,
+    row_ssem,
+    row_rsem,
+    col_ssem,
+    col_rsem,
+    small_sem,
+    wout_sem,
+    rs_ssem,
+    rs_rsem,
+    ag_ssem,
+    ag_rsem,
+    att_ssem,
+    att_rsem,
+):
+    rows, cols, half = patches_ref.shape
+    tokens = rows * cols
+    group = 2 * tiles
+    pairs = group // 2
+    tile, col, core = lax.axis_index("tile"), lax.axis_index("col"), lax.axis_index("mp")
+    me = 2 * tile + col
+    other = 1 - core
+
+    local = [
+        pltpu.make_async_copy(patches_ref, pbuf.at[core], load_sem.at[0]),
+        pltpu.make_async_copy(qkv_ref.at[1], qkvw.at[1], load_sem.at[1]),
+        pltpu.make_async_copy(qkv_ref.at[2], qkvw.at[2], load_sem.at[2]),
+        pltpu.make_async_copy(qkv_ref.at[0], qkvw.at[0], load_sem.at[3]),
+        pltpu.make_async_copy(
+            outw_ref.at[:, pl.ds(pl.multiple_of(core * half, half), half)],
+            wout.at[core],
+            load_sem.at[4],
+        ),
+    ]
+    for copy in local:
+        copy.start()
+
+    barrier = pltpu.get_barrier_semaphore()
+    for step in range(1, 2 * group):
+        peer = lax.rem(2 * me + core + step, 2 * group)
+        pl.semaphore_signal(
+            barrier,
+            inc=1,
+            device_id={"tile": peer // 4, "col": lax.rem(peer // 2, 2), "mp": lax.rem(peer, 2)},
+            device_id_type=MESH,
+        )
+    for tap in range(3):
+        small[core, 3 * tap : 3 * tap + 3, :] = conv_ref[tap].astype(F32)
+    small[core, 9:10, :] = gain_ref[...]
+    local[0].wait()
+    last = pbuf[core, :, 16:24, :].astype(F32)[:, 7:8, :]
+    first = pbuf[core, :, 0:8, :].astype(F32)[:, 0:1, :]
+    edge[...] = jnp.where(col == 0, last, first).reshape(rows, half).astype(BF16)
+    pl.semaphore_wait(barrier, 2 * group - 1)
+
+    above, below = tile > 0, tile < tiles - 1
+    side = {"col": 1 - col}
+
+    def row_copy(way, target):
+        return remote(
+            patches_ref.at[rows - 1 if way == 0 else 0],
+            rowh.at[core, way],
+            row_ssem.at[way, target],
+            row_rsem.at[core, way],
+            tile=tile + (1 if way == 0 else -1),
+            mp=core if target == 0 else other,
+        )
+
+    def col_copy(way, target):
+        return remote(
+            edge,
+            colh.at[core, way],
+            col_ssem.at[way, target],
+            col_rsem.at[core, way],
+            tile=tile + (0, 1, -1)[way],
+            mp=core if target == 0 else other,
+            **side,
+        )
+
+    for target in range(2):
+        for way, there in ((0, below), (1, above)):
+
+            @pl.when(there)
+            def _(way=way, target=target):
+                row_copy(way, target).start()
+                col_copy(way + 1, target).start()
+
+        col_copy(0, target).start()
+    patch_copy = remote(patches_ref, pbuf.at[core], patch_sem.at[0], patch_sem.at[1], mp=other)
+    patch_copy.start()
+    small_copy = remote(small.at[core], small.at[core], small_sem.at[0], small_sem.at[1], mp=other)
+    small_copy.start()
+    wout_copy = remote(
+        outw_ref.at[:, pl.ds(pl.multiple_of(other * half, half), half)],
+        wout.at[core],
+        wout_sem.at[0],
+        wout_sem.at[1],
+        mp=other,
+    )
+    wout_copy.start()
+
+    scaled = (omega_ref[...] * E ** (-0.25)).T
+    upper = scaled.astype(BF16)
+    lower = (scaled - upper.astype(F32)).astype(BF16)
+    sixteenth = jnp.full((E, M), -0.5 * E**-0.5, BF16)
+    lift[...] = jnp.zeros_like(lift)
+    for part, block in enumerate((upper, lower, sixteenth, sixteenth)):
+        for odd in range(2):
+            lift[128 * part + E * odd : 128 * part + E * odd + E, M * odd : M * odd + M] = block
+    rd[...] = jnp.zeros_like(rd)
+
+    row_of = lax.broadcasted_iota(jnp.int32, (rows, cols, rows), 0)
+    row_in = lax.broadcasted_iota(jnp.int32, (rows, cols, rows), 2)
+    col_of = lax.broadcasted_iota(jnp.int32, (rows, cols, cols), 1)
+    col_in = lax.broadcasted_iota(jnp.int32, (rows, cols, cols), 2)
+    pick_row = jnp.where(row_of == row_in, 1.0, 0.0).reshape(tokens, rows).astype(BF16)
+    pick_col = jnp.where(col_of == col_in, 1.0, 0.0).reshape(tokens, cols)
+    marks = jnp.dot(
+        pick_row, tissue_ref[...].astype(F32).astype(BF16), preferred_element_type=F32
+    )
+    keep[...] = jnp.dot(
+        (marks * pick_col).astype(BF16), jnp.ones((cols, 128), BF16), preferred_element_type=F32
+    )
+
+    def widen(slot):
+        start = pl.multiple_of(slot * half, half)
+        padded[1 : rows + 1, 8 : 8 + cols, pl.ds(start, half)] = pbuf[slot].astype(F32)
+
+    widen(core)
+    patch_copy.wait_recv()
+    widen(other)
+    for target in range(2):
+        slot = core if target == 0 else other
+        lanes = pl.ds(pl.multiple_of(slot * half, half), half)
+        remote(
+            edge, colh.at[slot, 0], col_ssem.at[0, 0], col_rsem.at[slot, 0], mp=other
+        ).wait_recv()
+        beside = colh[slot, 0].astype(F32)
+        zero = jnp.zeros_like(beside)
+        left = jnp.where(col == 1, beside, zero)
+        right = jnp.where(col == 0, beside, zero)
+        padded[1 : rows + 1, 7:8, lanes] = left.reshape(rows, 1, half)
+        padded[1 : rows + 1, 8 + cols : 9 + cols, lanes] = right.reshape(rows, 1, half)
+        for way, there in ((0, above), (1, below)):
+            line = 0 if way == 0 else rows + 1
+
+            @pl.when(there)
+            def _(way=way, slot=slot, lanes=lanes, line=line):
+                remote(
+                    patches_ref.at[0],
+                    rowh.at[slot, way],
+                    row_ssem.at[way, 0],
+                    row_rsem.at[slot, way],
+                    mp=other,
+                ).wait_recv()
+                remote(
+                    edge,
+                    colh.at[slot, way + 1],
+                    col_ssem.at[0, 0],
+                    col_rsem.at[slot, way + 1],
+                    mp=other,
+                ).wait_recv()
+                padded[line, 8 : 8 + cols, lanes] = rowh[slot, way].astype(F32)
+                at = rows - 1 if way == 0 else 0
+                corner = colh[slot, way + 1].astype(F32)[at : at + 1, :]
+                blank = jnp.zeros_like(corner)
+                padded[line, 7:8, lanes] = jnp.where(col == 1, corner, blank)
+                padded[line, 8 + cols : 9 + cols, lanes] = jnp.where(col == 0, corner, blank)
+
+            @pl.when(jnp.logical_not(there))
+            def _(lanes=lanes, line=line):
+                padded[line, :, lanes] = jnp.zeros((padded.shape[1], half), F32)
+
+    small_copy.wait_recv()
+
+    def stem_rows(step, carry):
+        line = 2 * step
+        here = pl.ds(pl.multiple_of(step * 2 * cols, 16), 2 * cols)
+        parts = []
+        for m in range(2):
+            lanes = slice(m * half, m * half + half)
+            total = padded[pl.ds(line + 1, 2), 8 : 8 + cols, lanes]
+            for a in range(3):
+                for b in range(3):
+                    total = total + small[m, 3 * a + b : 3 * a + b + 1, :].reshape(
+                        1, 1, half
+                    ) * padded[pl.ds(line + a, 2), 7 + b : 7 + b + cols, lanes]
+            flat = total.reshape(2 * cols, half)
+            stem[m, here, :] = flat
+            parts.append(flat)
+        width = 2 * half
+        mean_val = sum(jnp.sum(x, axis=1, keepdims=True) for x in parts) / width
+        square = sum(jnp.sum(x * x, axis=1, keepdims=True) for x in parts) / width
+        factor = lax.rsqrt(square - mean_val * mean_val + 1e-05)
+        for m in range(2):
+            nrm[here, m * half : m * half + half] = (
+                (parts[m] - mean_val) * factor * small[m, 9:10, :]
+            ).astype(BF16)
+        return carry
+
+    lax.fori_loop(0, rows // 2, stem_rows, 0)
+
+    def project(c):
+        return jnp.dot(nrm[...], qkvw[c], preferred_element_type=F32)
+
+    local[1].wait()
+    key = project(1)
+    for p in range(pairs):
+        kbuf[p] = key[:, 128 * p : 128 * p + 128].astype(BF16)
+    local[2].wait()
+    value = project(2)
+    for p in range(pairs):
+        vbuf[p] = (value[:, 128 * p : 128 * p + 128] * keep[...]).astype(BF16)
+
+    def phi(pair):
+        wide = pair.astype(F32)
+        square = wide * wide
+        high = square.astype(BF16)
+        low = (square - high.astype(F32)).astype(BF16)
+        joined = jnp.concatenate([pair, pair, high, low], axis=1)
+        lifted = jnp.dot(joined, lift[...], preferred_element_type=F32)
+        return (jnp.exp(lifted) * (1.0 / math.sqrt(M))).astype(BF16)
+
+    def share(h):
+        return remote(
+            rs_send.at[h],
+            rs_recv.at[me],
+            rs_ssem.at[h],
+            rs_rsem.at[me],
+            tile=h // 2,
+            col=lax.rem(h, 2),
+        )
+
+    def key_pair(step, carry):
+        p = lax.rem(step + tile, pairs)
+        feat = phi(kbuf[p])
+        left = jnp.concatenate([vbuf[p], keep[...].astype(BF16)], axis=1)
+        state = lax.dot_general(left, feat, (((0,), (0,)), ((), ())), preferred_element_type=F32)
+        for odd in range(2):
+            h = 2 * p + odd
+            rs_send[h, 0:E, :] = state[E * odd : E * odd + E, M * odd : M * odd + M].astype(BF16)
+            rs_send[h, E : E + 16, :] = state[128:144, M * odd : M * odd + M].astype(BF16)
+
+            @pl.when(h != me)
+            def _(h=h):
+                share(h).start()
+
+        return carry
+
+    lax.fori_loop(0, pairs, key_pair, 0)
+
+    local[3].wait()
+    query = project(0)
+    for p in range(pairs):
+        qbuf[p] = query[:, 128 * p : 128 * p + 128].astype(BF16)
+
+    def query_pair(p, carry):
+        qfb[p] = phi(qbuf[p])
+        return carry
+
+    lax.fori_loop(0, pairs // 2, query_pair, 0)
+
+    total = rs_send[me].astype(F32)
+    for step in range(1, group):
+        source = lax.rem(me + step, group)
+        remote(
+            rs_send.at[0], rs_recv.at[source], rs_ssem.at[0], rs_rsem.at[source], mp=other
+        ).wait_recv()
+        total = total + rs_recv[source].astype(F32)
+    ag[me] = total.astype(BF16)
+
+    def spread(step):
+        peer = lax.rem(me + step, group)
+        return remote(
+            ag.at[me],
+            ag.at[me],
+            ag_ssem.at[step],
+            ag_rsem.at[me],
+            tile=peer // 2,
+            col=lax.rem(peer, 2),
+        )
+
+    for step in range(1, group):
+        spread(step).start()
+
+    lax.fori_loop(pairs // 2, pairs, query_pair, 0)
+
+    def att_copy(p):
+        return remote(
+            att.at[core, p], att.at[core, p], att_ssem.at[p], att_rsem.at[core, p], mp=other
+        )
+
+    def read_pair(step, carry):
+        p = lax.rem(step + tile, pairs)
+        for odd in range(2):
+            h = 2 * p + odd
+
+            @pl.when(h != me)
+            def _(h=h):
+                remote(
+                    ag.at[h], ag.at[h], ag_ssem.at[0], ag_rsem.at[h], mp=other
+                ).wait_recv()
+
+            rd[E * odd : E * odd + E, M * odd : M * odd + M] = ag[h, 0:E, :]
+            norm = ag[h, E : E + 16, :]
+            for k in range(4):
+                at = 128 + E * odd + 16 * k
+                rd[at : at + 16, M * odd : M * odd + M] = norm
+        both = lax.dot_general(
+            qfb[p], rd[...], (((1,), (1,)), ((), ())), preferred_element_type=F32
+        )
+        att[core, p] = (both[:, :128] / both[:, 128:]).astype(BF16)
+        att_copy(p).start()
+        return carry
+
+    lax.fori_loop(0, pairs, read_pair, 0)
+
+    def mix(slot):
+        return jnp.dot(
+            jnp.concatenate([att[slot, p] for p in range(pairs)], axis=1),
+            wout[slot],
+            preferred_element_type=F32,
+        )
+
+    local[4].wait()
+    stem[core] = stem[core] + mix(core)
+    wout_copy.wait_recv()
+    for p in range(pairs):
+        remote(
+            att.at[core, p], att.at[other, p], att_ssem.at[p], att_rsem.at[other, p], mp=other
+        ).wait_recv()
+    result = stem[core] + mix(other)
+    out_ref[...] = result.reshape(rows, cols, half).astype(BF16)
+
+    for target in range(2):
+        for way, there in ((0, below), (1, above)):
+
+            @pl.when(there)
+            def _(way=way, target=target):
+                row_copy(way, target).wait_send()
+                col_copy(way + 1, target).wait_send()
+
+        col_copy(0, target).wait_send()
+    for copy in (patch_copy, small_copy, wout_copy):
+        copy.wait_send()
+
+    def drain(h, carry):
+        @pl.when(h != me)
+        def _():
+            share(h).wait_send()
+
+        return carry
+
+    lax.fori_loop(0, group, drain, 0)
+    for step in range(1, group):
+        spread(step).wait_send()
+    for p in range(pairs):
+        att_copy(p).wait_send()
+
+
+def fused(tiles, patches, tissue, conv_weight, ln_gain, qkv_weight, omega, out_weight):
+    rows, cols, half = patches.shape
+    tokens = rows * cols
+    group = 2 * tiles
+    pairs = group // 2
+    vmem, dma = pltpu.VMEM, pltpu.SemaphoreType.DMA
+    anywhere = pl.BlockSpec(memory_space=pl.ANY)
+    inside = pl.BlockSpec(memory_space=pltpu.VMEM)
+    return pl.pallas_call(
+        functools.partial(layer_kernel, tiles),
+        out_shape=jax.ShapeDtypeStruct(patches.shape, BF16),
+        in_specs=[anywhere, inside, inside, inside, anywhere, inside, anywhere],
+        out_specs=inside,
+        scratch_shapes=[
+            vmem((2, rows, cols, half), BF16),
+            vmem((rows + 2, cols + 16, 2 * half), F32),
+            vmem((2, 2, cols, half), BF16),
+            vmem((2, 3, rows, half), BF16),
+            vmem((rows, half), BF16),
+            vmem((2, 16, half), F32),
+            vmem(qkv_weight.shape, BF16),
+            vmem((2, half, half), BF16),
+            vmem((2, tokens, half), F32),
+            vmem((tokens, 2 * half), BF16),
+            vmem((tokens, 128), F32),
+            vmem((512, 2 * M), BF16),
+            vmem((pairs, tokens, 128), BF16),
+            vmem((pairs, tokens, 128), BF16),
+            vmem((pairs, tokens, 128), BF16),
+            vmem((pairs, tokens, 2 * M), BF16),
+            vmem((group, E + 16, M), BF16),
+            vmem((group, E + 16, M), BF16),
+            vmem((group, E + 16, M), BF16),
+            vmem((256, 2 * M), BF16),
+            vmem((2, pairs, tokens, 128), BF16),
+            dma((5,)),
+            dma((2,)),
+            dma((2, 2)),
+            dma((2, 2)),
+            dma((3, 2)),
+            dma((2, 3)),
+            dma((2,)),
+            dma((2,)),
+            dma((group,)),
+            dma((group,)),
+            dma((group,)),
+            dma((group,)),
+            dma((pairs,)),
+            dma((2, pairs)),
+        ],
+        compiler_params=pltpu.CompilerParams(
+            collective_id=0, has_side_effects=True, vmem_limit_bytes=48 * 2**20
+        ),
+    )(patches, tissue, conv_weight, ln_gain.reshape(1, half), qkv_weight, omega, out_weight)
+
+
 def solution(mesh):
+    tiles, sides, cores = mesh.shape["tile"], mesh.shape["col"], mesh.shape["mp"]
+
+    def body(*args):
+        heads_here = args[4].shape[2] // E
+        if sides == 2 and cores == 2 and tiles * sides == heads_here:
+            return fused(tiles, *args)
+        return shards(*args)
+
     placed = (
         P(("slides", "tile"), "col", "mp"),
         P(("slides", "tile"), "col"),
@@ -114,7 +583,7 @@
         P("mp", None),
     )
     return jax.shard_map(
-        shards,
+        body,
         mesh=mesh,
         in_specs=placed,
         out_specs=P(("slides", "tile"), "col", "mp"),

time: 168 us -> 42.4 us (0.25)
  waiting for transfers between devices: 77.8 us -> 0 us
  Pallas kernels: 0 us -> 34.1 us
  blocking collectives: 20.7 us -> 0 us
  matrix products: 19.5 us -> 0 us
  between operations: 13.8 us -> 0.03 us
  other arithmetic: 10.9 us -> 0 us
  starting transfers between devices: 10.6 us -> 0 us
  local copies, waits for them, and re-layouts: 13 us -> 7.87 us
    psum x1 -> x0, waiting for transfers between devices: 65.6 us -> none  [shards(): kv_state, normalizer = lax.psum((state, key_sum), ('tile', 'col'))]
    pallas_call x0 -> x1, Pallas kernels: none -> 34.1 us  [fused(): pl.pallas_call(functools.partial(layer_kernel, tiles), out_shape=jax.Shap...]
    dot_general x9 -> x0, matrix products: 19.5 us -> none  [the longest x2 10.1 us: features(): jnp.einsum('the,me->thm', scaled, omega, precision=lax.Precision.HIGHEST)]
    psum x2 -> x0, blocking collectives: 18.3 us -> none  [the longest x1 13.1 us: shards(): kv_state, normalizer = lax.psum((state, key_sum), ('tile', 'col'))]
    reduce_scatter x1 -> x0, waiting for transfers between devices: 11.3 us -> none  [shards(): lax.psum_scatter(lax.dot_general(out_weight, attended, (((0,), (1,)), (()...]
    ppermute x4 -> x0, starting transfers between devices: 10.4 us -> none  [the longest x2 5.27 us: extended(): lax.ppermute(head, axis, [((i + 1) % count, i) for i in range(ends)])]
    convert_element_type x5 -> x0, other arithmetic: 5.37 us -> none  [the longest x1 2.1 us: shards(): (flat + mixed).astype(jnp.bfloat16).reshape(rows_here, cols_here, half)]
    unnamed x38 -> x14, local copies, waits for them, and re-layouts: 2.58 us -> 7.87 us
  transfers between devices with their start and end apart: 6 -> 0, of which waited for: 3 -> 0; matrix products, arithmetic and copies ran while one was open for 8% -> 0% of each run, Pallas kernels for 0% -> 0%
where the time goes in v1:
time: 42.4 us; the launch traced here: 42 us
  Pallas kernels  34.1 us (80%)
  local copies, waits for them, and re-layouts  7.87 us (19%)
    pallas_call x1, Pallas kernels, fused(): pl.pallas_call(functools.partial(layer_kernel, tiles), out_shape=jax.Shap...  34.1 us
    unnamed x14, local copies, waits for them, and re-layouts  7.87 us

profile of v1, /device:TPU:29, one launch (start us, length us, event | category | flops | bytes accessed | tf_op | source)
XLA Modules:
  0.0 42.0 jit_solution(11046387485271263120)
XLA Ops:
  0.0 0.9 %copy.8.omega_ref = f32[256,64]{1,0:T(8,128)S(1)} copy(f32[256,64]{0,1:T(8,128)} %param.12) | data formatting | bytes 131072 | tf_op args[5]
  0.9 0.0 copy-start
  0.9 1.9 %copy-done = bf16[3,1024,512]{2,1,0:T(8,128)(2,1)S(1)} copy-done((bf16[3,1024,512]{2,1,0:T(8,128)(2,1)S(1)}, bf16[3,1024,512]{2,1,0:T(8,128)(2,1)}, u32[]{:S(2)}) %copy-start) | copy-done | bytes 3145752
  2.8 0.0 copy-start.1
  2.8 1.2 %copy-done.1 = bf16[512,1024]{1,0:T(8,128)(2,1)S(1)} copy-done((bf16[512,1024]{1,0:T(8,128)(2,1)S(1)}, bf16[512,1024]{1,0:T(8,128)(2,1)}, u32[]{:S(2)}) %copy-start.1) | copy-done | bytes 1048600
  4.1 0.0 copy-start.2
  4.1 1.0 %copy-done.2 = bf16[16,24,512]{2,1,0:T(8,128)(2,1)S(1)} copy-done((bf16[16,24,512]{2,1,0:T(8,128)(2,1)S(1)}, bf16[16,24,512]{2,1,0:T(8,128)(2,1)}, u32[]{:S(2)}) %copy-start.2) | copy-done | bytes 393240
  5.1 0.0 copy-start.3
  5.1 0.7 %copy-done.3 = bf16[3,3,512]{2,1,0:T(4,128)(2,1)S(1)} copy-done((bf16[3,3,512]{2,1,0:T(4,128)(2,1)S(1)}, bf16[3,3,512]{2,1,0:T(4,128)(2,1)}, u32[]{:S(2)}) %copy-start.3) | copy-done | bytes 9240
  5.8 0.0 copy-start.4
  5.8 0.7 %copy-done.4 = s32[16,24]{1,0:T(8,128)S(1)} copy-done((s32[16,24]{1,0:T(8,128)S(1)}, s32[16,24]{1,0:T(8,128)}, u32[]{:S(2)}) %copy-start.4) | copy-done | bytes 1560
  6.5 0.0 copy-start.5
  6.5 0.7 %copy-done.5 = f32[512]{0:T(512)S(1)} copy-done((f32[512]{0:T(512)S(1)}, f32[512]{0:T(512)}, u32[]{:S(2)}) %copy-start.5) | copy-done | bytes 2072
  7.1 34.1 %shard_map.73 = bf16[16,24,512]{2,1,0:T(8,128)(2,1)S(1)} custom-call(bf16[16,24,512]{2,1,0:T(8,128)(2,1)S(1)} %copy-done.2, s32[16,24]{1,0:T(8,128)S(1)} %copy-done.4, bf16[3,3,512]{2,1,0:T(4,128)(2,1)S(1)} %copy-done.3, f32[1,512]{1,0:T(1,128)S(1)} %bitcast.1, bf16[3,1024,512]{2,1,0:T(8,128)(2,1)S(1)} %copy-done, f32[256,64]{1,0:T(8,128)S(1)} %copy.8.omega_ref, ...), custom_call_target="tpu_custom_call" | custom-call | tf_op jit(solution)/shard_map/pallas_call | solution.py:519
  41.3 0.7 %copy.10 = bf16[16,24,512]{2,1,0:T(8,128)(2,1)} copy(bf16[16,24,512]{2,1,0:T(8,128)(2,1)S(1)} %shard_map.73) | data formatting | bytes 786432
Async XLA Ops:
  0.9 1.9 %copy-start = (bf16[3,1024,512]{2,1,0:T(8,128)(2,1)S(1)}, bf16[3,1024,512]{2,1,0:T(8,128)(2,1)}, u32[]{:S(2)}) copy-start(bf16[3,1024,512]{2,1,0:T(8,128)(2,1)} %qkv_ref.1) | copy-start | bytes 9437188
  2.8 1.2 %copy-start.1 = (bf16[512,1024]{1,0:T(8,128)(2,1)S(1)}, bf16[512,1024]{1,0:T(8,128)(2,1)}, u32[]{:S(2)}) copy-start(bf16[512,1024]{1,0:T(8,128)(2,1)} %outw_ref.1) | copy-start | bytes 3145732
  4.1 1.0 %copy-start.2 = (bf16[16,24,512]{2,1,0:T(8,128)(2,1)S(1)}, bf16[16,24,512]{2,1,0:T(8,128)(2,1)}, u32[]{:S(2)}) copy-start(bf16[16,24,512]{2,1,0:T(8,128)(2,1)} %patches_ref.1) | copy-start | bytes 1179652
  5.1 0.7 %copy-start.3 = (bf16[3,3,512]{2,1,0:T(4,128)(2,1)S(1)}, bf16[3,3,512]{2,1,0:T(4,128)(2,1)}, u32[]{:S(2)}) copy-start(bf16[3,3,512]{2,1,0:T(4,128)(2,1)} %conv_ref.1) | copy-start | bytes 27652
  5.8 0.7 %copy-start.4 = (s32[16,24]{1,0:T(8,128)S(1)}, s32[16,24]{1,0:T(8,128)}, u32[]{:S(2)}) copy-start(s32[16,24]{1,0:T(8,128)} %tissue_ref.1) | copy-start | bytes 4612
  6.5 0.7 %copy-start.5 = (f32[512]{0:T(512)S(1)}, f32[512]{0:T(512)}, u32[]{:S(2)}) copy-start(f32[512]{0:T(512)} %param.10) | copy-start | bytes 6148

commit v2 on v1

--- a/solution.py
+++ b/solution.py
@@ -120,13 +120,17 @@
 def layer_kernel(
     tiles,
     patches_ref,
+    tissue_hbm,
+    conv_hbm,
+    gain_hbm,
+    qkv_ref,
+    omega_hbm,
+    outw_ref,
+    out_ref,
     tissue_ref,
     conv_ref,
     gain_ref,
-    qkv_ref,
     omega_ref,
-    outw_ref,
-    out_ref,
     pbuf,
     padded,
     rowh,
@@ -144,7 +148,9 @@
     qbuf,
     qfb,
     rs_send,
-    rs_recv,
+    xr,
+    zs,
+    zr,
     ag,
     rd,
     att,
@@ -156,9 +162,12 @@
     col_rsem,
     small_sem,
     wout_sem,
-    rs_ssem,
-    rs_rsem,
+    x_ssem,
+    x_rsem,
+    z_ssem,
+    z_rsem,
     ag_ssem,
+    fw_ssem,
     ag_rsem,
     att_ssem,
     att_rsem,
@@ -181,9 +190,13 @@
             wout.at[core],
             load_sem.at[4],
         ),
+        pltpu.make_async_copy(conv_hbm, conv_ref, load_sem.at[5]),
+        pltpu.make_async_copy(gain_hbm, gain_ref, load_sem.at[6]),
+        pltpu.make_async_copy(omega_hbm, omega_ref, load_sem.at[7]),
+        pltpu.make_async_copy(tissue_hbm, tissue_ref, load_sem.at[8]),
     ]
-    for copy in local:
-        copy.start()
+    for index in (0, 5, 6, 7, 8, 1, 2, 3, 4):
+        local[index].start()
 
     barrier = pltpu.get_barrier_semaphore()
     for step in range(1, 2 * group):
@@ -194,6 +207,8 @@
             device_id={"tile": peer // 4, "col": lax.rem(peer // 2, 2), "mp": lax.rem(peer, 2)},
             device_id_type=MESH,
         )
+    local[5].wait()
+    local[6].wait()
     for tap in range(3):
         small[core, 3 * tap : 3 * tap + 3, :] = conv_ref[tap].astype(F32)
     small[core, 9:10, :] = gain_ref[...]
@@ -249,7 +264,8 @@
     )
     wout_copy.start()
 
-    scaled = (omega_ref[...] * E ** (-0.25)).T
+    local[7].wait()
+    scaled = omega_ref[...] * E ** (-0.25)
     upper = scaled.astype(BF16)
     lower = (scaled - upper.astype(F32)).astype(BF16)
     sixteenth = jnp.full((E, M), -0.5 * E**-0.5, BF16)
@@ -259,6 +275,7 @@
             lift[128 * part + E * odd : 128 * part + E * odd + E, M * odd : M * odd + M] = block
     rd[...] = jnp.zeros_like(rd)
 
+    local[8].wait()
     row_of = lax.broadcasted_iota(jnp.int32, (rows, cols, rows), 0)
     row_in = lax.broadcasted_iota(jnp.int32, (rows, cols, rows), 2)
     col_of = lax.broadcasted_iota(jnp.int32, (rows, cols, cols), 1)
@@ -371,18 +388,16 @@
         lifted = jnp.dot(joined, lift[...], preferred_element_type=F32)
         return (jnp.exp(lifted) * (1.0 / math.sqrt(M))).astype(BF16)
 
-    def share(h):
+    def across(p):
         return remote(
-            rs_send.at[h],
-            rs_recv.at[me],
-            rs_ssem.at[h],
-            rs_rsem.at[me],
-            tile=h // 2,
-            col=lax.rem(h, 2),
-        )
+            rs_send.at[2 * p + 1 - col], xr.at[p], x_ssem.at[p], x_rsem.at[p], col=1 - col
+        )
+
+    def along(p):
+        return remote(zs.at[p], zr.at[tile], z_ssem.at[p], z_rsem.at[tile], tile=p)
 
     def key_pair(step, carry):
-        p = lax.rem(step + tile, pairs)
+        p = lax.rem(step + 1 + tile, pairs)
         feat = phi(kbuf[p])
         left = jnp.concatenate([vbuf[p], keep[...].astype(BF16)], axis=1)
         state = lax.dot_general(left, feat, (((0,), (0,)), ((), ())), preferred_element_type=F32)
@@ -390,11 +405,7 @@
             h = 2 * p + odd
             rs_send[h, 0:E, :] = state[E * odd : E * odd + E, M * odd : M * odd + M].astype(BF16)
             rs_send[h, E : E + 16, :] = state[128:144, M * odd : M * odd + M].astype(BF16)
-
-            @pl.when(h != me)
-            def _(h=h):
-                share(h).start()
-
+        across(p).start()
         return carry
 
     lax.fori_loop(0, pairs, key_pair, 0)
@@ -408,30 +419,49 @@
         qfb[p] = phi(qbuf[p])
         return carry
 
+
+    def fold_pair(step, carry):
+        p = lax.rem(step + 1 + tile, pairs)
+        across(p).wait_recv()
+        zs[p] = (rs_send[2 * p + col].astype(F32) + xr[p].astype(F32)).astype(BF16)
+
+        @pl.when(p != tile)
+        def _():
+            along(p).start()
+
+        return carry
+
+    lax.fori_loop(0, pairs, fold_pair, 0)
     lax.fori_loop(0, pairs // 2, query_pair, 0)
 
-    total = rs_send[me].astype(F32)
-    for step in range(1, group):
-        source = lax.rem(me + step, group)
+    total = zs[tile].astype(F32)
+    for step in range(1, tiles):
+        source = lax.rem(tile + step, tiles)
         remote(
-            rs_send.at[0], rs_recv.at[source], rs_ssem.at[0], rs_rsem.at[source], mp=other
+            zs.at[0], zr.at[source], z_ssem.at[0], z_rsem.at[source], mp=other
         ).wait_recv()
-        total = total + rs_recv[source].astype(F32)
+        total = total + zr[source].astype(F32)
     ag[me] = total.astype(BF16)
 
     def spread(step):
-        peer = lax.rem(me + step, group)
         return remote(
             ag.at[me],
             ag.at[me],
             ag_ssem.at[step],
             ag_rsem.at[me],
-            tile=peer // 2,
-            col=lax.rem(peer, 2),
-        )
-
-    for step in range(1, group):
+            tile=lax.rem(tile + step, tiles),
+        )
+
+    def forward(p):
+        h = 2 * p + col
+        return remote(ag.at[h], ag.at[h], fw_ssem.at[p], ag_rsem.at[h], col=1 - col)
+
+    def arrived(h):
+        remote(ag.at[h], ag.at[h], ag_ssem.at[0], ag_rsem.at[h], mp=other).wait_recv()
+
+    for step in range(1, tiles):
         spread(step).start()
+    forward(tile).start()
 
     lax.fori_loop(pairs // 2, pairs, query_pair, 0)
 
@@ -442,15 +472,16 @@
 
     def read_pair(step, carry):
         p = lax.rem(step + tile, pairs)
+        later = lax.rem(p + 1, pairs)
+
+        @pl.when(step < pairs - 1)
+        def _():
+            arrived(2 * later + col)
+            forward(later).start()
+
+        arrived(2 * p + 1 - col)
         for odd in range(2):
             h = 2 * p + odd
-
-            @pl.when(h != me)
-            def _(h=h):
-                remote(
-                    ag.at[h], ag.at[h], ag_ssem.at[0], ag_rsem.at[h], mp=other
-                ).wait_recv()
-
             rd[E * odd : E * odd + E, M * odd : M * odd + M] = ag[h, 0:E, :]
             norm = ag[h, E : E + 16, :]
             for k in range(4):
@@ -494,16 +525,12 @@
     for copy in (patch_copy, small_copy, wout_copy):
         copy.wait_send()
 
-    def drain(h, carry):
-        @pl.when(h != me)
-        def _():
-            share(h).wait_send()
-
-        return carry
-
-    lax.fori_loop(0, group, drain, 0)
-    for step in range(1, group):
+    for step in range(1, tiles):
         spread(step).wait_send()
+        along(lax.rem(tile + step, tiles)).wait_send()
+    for p in range(pairs):
+        across(p).wait_send()
+        forward(p).wait_send()
     for p in range(pairs):
         att_copy(p).wait_send()
 
@@ -519,9 +546,13 @@
     return pl.pallas_call(
         functools.partial(layer_kernel, tiles),
         out_shape=jax.ShapeDtypeStruct(patches.shape, BF16),
-        in_specs=[anywhere, inside, inside, inside, anywhere, inside, anywhere],
+        in_specs=[anywhere] * 7,
         out_specs=inside,
         scratch_shapes=[
+            vmem(tissue.shape, jnp.int32),
+            vmem(conv_weight.shape, BF16),
+            vmem((1, half), F32),
+            vmem((E, M), F32),
             vmem((2, rows, cols, half), BF16),
             vmem((rows + 2, cols + 16, 2 * half), F32),
             vmem((2, 2, cols, half), BF16),
@@ -539,11 +570,13 @@
             vmem((pairs, tokens, 128), BF16),
             vmem((pairs, tokens, 2 * M), BF16),
             vmem((group, E + 16, M), BF16),
-            vmem((group, E + 16, M), BF16),
+            vmem((pairs, E + 16, M), BF16),
+            vmem((pairs, E + 16, M), BF16),
+            vmem((tiles, E + 16, M), BF16),
             vmem((group, E + 16, M), BF16),
             vmem((256, 2 * M), BF16),
             vmem((2, pairs, tokens, 128), BF16),
-            dma((5,)),
+            dma((9,)),
             dma((2,)),
             dma((2, 2)),
             dma((2, 2)),
@@ -551,17 +584,20 @@
             dma((2, 3)),
             dma((2,)),
             dma((2,)),
-            dma((group,)),
-            dma((group,)),
-            dma((group,)),
+            dma((pairs,)),
+            dma((pairs,)),
+            dma((pairs,)),
+            dma((tiles,)),
+            dma((tiles,)),
+            dma((pairs,)),
             dma((group,)),
             dma((pairs,)),
             dma((2, pairs)),
         ],
         compiler_params=pltpu.CompilerParams(
-            collective_id=0, has_side_effects=True, vmem_limit_bytes=48 * 2**20
+            collective_id=0, has_side_effects=True, vmem_limit_bytes=63 * 2**20
         ),
-    )(patches, tissue, conv_weight, ln_gain.reshape(1, half), qkv_weight, omega, out_weight)
+    )(patches, tissue, conv_weight, ln_gain.reshape(1, half), qkv_weight, omega.T, out_weight)
 
 
 def solution(mesh):

time: 42.4 us -> 37.9 us (0.89)
  local copies, waits for them, and re-layouts: 7.87 us -> 1.77 us
  Pallas kernels: 34.1 us -> 35.6 us
    unnamed x14 -> x1, local copies, waits for them, and re-layouts: 7.87 us -> 1.77 us
    pallas_call x1, Pallas kernels: 34.1 us -> 35.6 us  [fused(): pl.pallas_call(functools.partial(layer_kernel, tiles), out_shape=jax.Shap...]
where the time goes in v2:
time: 37.9 us; the launch traced here: 37.3 us
  Pallas kernels  35.6 us (94%)
  local copies, waits for them, and re-layouts  1.77 us (5%)
    pallas_call x1, Pallas kernels, fused(): pl.pallas_call(functools.partial(layer_kernel, tiles), out_shape=jax.Shap...  35.6 us
    unnamed x1, local copies, waits for them, and re-layouts  1.77 us

profile of v2, /device:TPU:29, one launch (start us, length us, event | category | flops | bytes accessed | tf_op | source)
XLA Modules:
  0.0 37.3 jit_solution(11602605952973611662)
XLA Ops:
  0.0 35.6 %shard_map.73 = bf16[16,24,512]{2,1,0:T(8,128)(2,1)} custom-call(bf16[16,24,512]{2,1,0:T(8,128)(2,1)} %patches_ref.1, s32[16,24]{1,0:T(8,128)} %tissue_hbm.1, bf16[3,3,512]{2,1,0:T(4,128)(2,1)} %conv_hbm.1, f32[1,512]{1,0:T(1,128)} %bitcast.3, bf16[3,1024,512]{2,1,0:T(8,128)(2,1)} %qkv_ref.1, f32[64,256]{1,0:T(8,128)} %bitcast.2, bf16[512,1024]{1,0:T(8,128)(2,1)} %outw_ref.1), custom_call_target="tpu_custom_call" | custom-call | tf_op jit(solution)/shard_map/pallas_call | solution.py:546
  35.6 1.8 %copy.9 = bf16[16,24,512]{2,1,0:T(8,128)(2,1)} copy(bf16[16,24,512]{2,1,0:T(8,128)(2,1)} %shard_map.73) | data formatting | bytes 786432

commit v3 on v1

--- a/solution.py
+++ b/solution.py
@@ -120,13 +120,17 @@
 def layer_kernel(
     tiles,
     patches_ref,
+    tissue_hbm,
+    conv_hbm,
+    gain_hbm,
+    qkv_ref,
+    omega_hbm,
+    outw_ref,
+    out_ref,
     tissue_ref,
     conv_ref,
     gain_ref,
-    qkv_ref,
     omega_ref,
-    outw_ref,
-    out_ref,
     pbuf,
     padded,
     rowh,
@@ -146,6 +150,8 @@
     rs_send,
     rs_recv,
     ag,
+    norms,
+    norms_all,
     rd,
     att,
     load_sem,
@@ -162,6 +168,8 @@
     ag_rsem,
     att_ssem,
     att_rsem,
+    nz_ssem,
+    nz_rsem,
 ):
     rows, cols, half = patches_ref.shape
     tokens = rows * cols
@@ -181,9 +189,13 @@
             wout.at[core],
             load_sem.at[4],
         ),
+        pltpu.make_async_copy(conv_hbm, conv_ref, load_sem.at[5]),
+        pltpu.make_async_copy(gain_hbm, gain_ref, load_sem.at[6]),
+        pltpu.make_async_copy(omega_hbm, omega_ref, load_sem.at[7]),
+        pltpu.make_async_copy(tissue_hbm, tissue_ref, load_sem.at[8]),
     ]
-    for copy in local:
-        copy.start()
+    for index in (0, 5, 6, 7, 8, 1, 2, 3, 4):
+        local[index].start()
 
     barrier = pltpu.get_barrier_semaphore()
     for step in range(1, 2 * group):
@@ -194,6 +206,8 @@
             device_id={"tile": peer // 4, "col": lax.rem(peer // 2, 2), "mp": lax.rem(peer, 2)},
             device_id_type=MESH,
         )
+    local[5].wait()
+    local[6].wait()
     for tap in range(3):
         small[core, 3 * tap : 3 * tap + 3, :] = conv_ref[tap].astype(F32)
     small[core, 9:10, :] = gain_ref[...]
@@ -249,7 +263,8 @@
     )
     wout_copy.start()
 
-    scaled = (omega_ref[...] * E ** (-0.25)).T
+    local[7].wait()
+    scaled = omega_ref[...] * E ** (-0.25)
     upper = scaled.astype(BF16)
     lower = (scaled - upper.astype(F32)).astype(BF16)
     sixteenth = jnp.full((E, M), -0.5 * E**-0.5, BF16)
@@ -259,6 +274,7 @@
             lift[128 * part + E * odd : 128 * part + E * odd + E, M * odd : M * odd + M] = block
     rd[...] = jnp.zeros_like(rd)
 
+    local[8].wait()
     row_of = lax.broadcasted_iota(jnp.int32, (rows, cols, rows), 0)
     row_in = lax.broadcasted_iota(jnp.int32, (rows, cols, rows), 2)
     col_of = lax.broadcasted_iota(jnp.int32, (rows, cols, cols), 1)
@@ -382,14 +398,14 @@
         )
 
     def key_pair(step, carry):
-        p = lax.rem(step + tile, pairs)
+        p = lax.rem(step + 1 + tile, pairs)
         feat = phi(kbuf[p])
         left = jnp.concatenate([vbuf[p], keep[...].astype(BF16)], axis=1)
         state = lax.dot_general(left, feat, (((0,), (0,)), ((), ())), preferred_element_type=F32)
         for odd in range(2):
             h = 2 * p + odd
-            rs_send[h, 0:E, :] = state[E * odd : E * odd + E, M * odd : M * odd + M].astype(BF16)
-            rs_send[h, E : E + 16, :] = state[128:144, M * odd : M * odd + M].astype(BF16)
+            rs_send[h] = state[E * odd : E * odd + E, M * odd : M * odd + M].astype(BF16)
+            norms[pl.ds(h, 1), :] = state[128:129, M * odd : M * odd + M]
 
             @pl.when(h != me)
             def _(h=h):
@@ -398,7 +414,21 @@
         return carry
 
     lax.fori_loop(0, pairs, key_pair, 0)
-
+    norms_all[me] = norms[...]
+
+    def norm_share(step):
+        peer = lax.rem(me + step, group)
+        return remote(
+            norms_all.at[me],
+            norms_all.at[me],
+            nz_ssem.at[step],
+            nz_rsem.at[me],
+            tile=peer // 2,
+            col=lax.rem(peer, 2),
+        )
+
+    for step in range(1, group):
+        norm_share(step).start()
     local[3].wait()
     query = project(0)
     for p in range(pairs):
@@ -408,7 +438,8 @@
         qfb[p] = phi(qbuf[p])
         return carry
 
-    lax.fori_loop(0, pairs // 2, query_pair, 0)
+
+    lax.fori_loop(0, pairs - 1, query_pair, 0)
 
     total = rs_send[me].astype(F32)
     for step in range(1, group):
@@ -430,10 +461,19 @@
             col=lax.rem(peer, 2),
         )
 
+    def arrived(h):
+        remote(ag.at[h], ag.at[h], ag_ssem.at[0], ag_rsem.at[h], mp=other).wait_recv()
+
     for step in range(1, group):
         spread(step).start()
 
-    lax.fori_loop(pairs // 2, pairs, query_pair, 0)
+    query_pair(pairs - 1, 0)
+    for step in range(1, group):
+        source = lax.rem(me + step, group)
+        remote(
+            norms_all.at[0], norms_all.at[source], nz_ssem.at[0], nz_rsem.at[source], mp=other
+        ).wait_recv()
+    norms[...] = sum(norms_all[s] for s in range(group))
 
     def att_copy(p):
         return remote(
@@ -447,15 +487,12 @@
 
             @pl.when(h != me)
             def _(h=h):
-                remote(
-                    ag.at[h], ag.at[h], ag_ssem.at[0], ag_rsem.at[h], mp=other
-                ).wait_recv()
-
-            rd[E * odd : E * odd + E, M * odd : M * odd + M] = ag[h, 0:E, :]
-            norm = ag[h, E : E + 16, :]
-            for k in range(4):
-                at = 128 + E * odd + 16 * k
-                rd[at : at + 16, M * odd : M * odd + M] = norm
+                arrived(h)
+
+            rd[E * odd : E * odd + E, M * odd : M * odd + M] = ag[h]
+            rd[128 + E * odd : 128 + E * odd + E, M * odd : M * odd + M] = jnp.broadcast_to(
+                norms[pl.ds(h, 1), :], (E, M)
+            ).astype(BF16)
         both = lax.dot_general(
             qfb[p], rd[...], (((1,), (1,)), ((), ())), preferred_element_type=F32
         )
@@ -504,6 +541,7 @@
     lax.fori_loop(0, group, drain, 0)
     for step in range(1, group):
         spread(step).wait_send()
+        norm_share(step).wait_send()
     for p in range(pairs):
         att_copy(p).wait_send()
 
@@ -518,10 +556,14 @@
     inside = pl.BlockSpec(memory_space=pltpu.VMEM)
     return pl.pallas_call(
         functools.partial(layer_kernel, tiles),
-        out_shape=jax.ShapeDtypeStruct(patches.shape, BF16),
-        in_specs=[anywhere, inside, inside, inside, anywhere, inside, anywhere],
+        out_shape=pltpu.VMEM(patches.shape, BF16),
+        in_specs=[anywhere] * 7,
         out_specs=inside,
         scratch_shapes=[
+            vmem(tissue.shape, jnp.int32),
+            vmem(conv_weight.shape, BF16),
+            vmem((1, half), F32),
+            vmem((E, M), F32),
             vmem((2, rows, cols, half), BF16),
             vmem((rows + 2, cols + 16, 2 * half), F32),
             vmem((2, 2, cols, half), BF16),
@@ -538,12 +580,14 @@
             vmem((pairs, tokens, 128), BF16),
             vmem((pairs, tokens, 128), BF16),
             vmem((pairs, tokens, 2 * M), BF16),
-            vmem((group, E + 16, M), BF16),
-            vmem((group, E + 16, M), BF16),
-            vmem((group, E + 16, M), BF16),
+            vmem((group, E, M), BF16),
+            vmem((group, E, M), BF16),
+            vmem((group, E, M), BF16),
+            vmem((group, M), F32),
+            vmem((group, group, M), F32),
             vmem((256, 2 * M), BF16),
             vmem((2, pairs, tokens, 128), BF16),
-            dma((5,)),
+            dma((9,)),
             dma((2,)),
             dma((2, 2)),
             dma((2, 2)),
@@ -557,11 +601,13 @@
             dma((group,)),
             dma((pairs,)),
             dma((2, pairs)),
+            dma((group,)),
+            dma((group,)),
         ],
         compiler_params=pltpu.CompilerParams(
-            collective_id=0, has_side_effects=True, vmem_limit_bytes=48 * 2**20
+            collective_id=0, has_side_effects=True, vmem_limit_bytes=63 * 2**20
         ),
-    )(patches, tissue, conv_weight, ln_gain.reshape(1, half), qkv_weight, omega, out_weight)
+    )(patches, tissue, conv_weight, ln_gain.reshape(1, half), qkv_weight, omega.T, out_weight)
 
 
 def solution(mesh):

time: 42.4 us -> 32.5 us (0.77)
  local copies, waits for them, and re-layouts: 7.87 us -> 0.75 us
  Pallas kernels: 34.1 us -> 31.6 us
    unnamed x14 -> x1, local copies, waits for them, and re-layouts: 7.87 us -> 0.75 us
    pallas_call x1, Pallas kernels: 34.1 us -> 31.6 us  [fused(): pl.pallas_call(functools.partial(layer_kernel, tiles), out_shape=pltpu.VM...]
where the time goes in v3:
time: 32.5 us; the launch traced here: 32.3 us
  Pallas kernels  31.6 us (97%)
  local copies, waits for them, and re-layouts  0.75 us (2%)
    pallas_call x1, Pallas kernels, fused(): pl.pallas_call(functools.partial(layer_kernel, tiles), out_shape=pltpu.VM...  31.6 us
    unnamed x1, local copies, waits for them, and re-layouts  0.75 us

profile of v3, /device:TPU:29, one launch (start us, length us, event | category | flops | bytes accessed | tf_op | source)
XLA Modules:
  0.0 32.3 jit_solution(464868387452193554)
XLA Ops:
  0.0 31.6 %shard_map.73 = bf16[16,24,512]{2,1,0:T(8,128)(2,1)S(1)} custom-call(bf16[16,24,512]{2,1,0:T(8,128)(2,1)} %patches_ref.1, s32[16,24]{1,0:T(8,128)} %tissue_hbm.1, bf16[3,3,512]{2,1,0:T(4,128)(2,1)} %conv_hbm.1, f32[1,512]{1,0:T(1,128)} %bitcast.3, bf16[3,1024,512]{2,1,0:T(8,128)(2,1)} %qkv_ref.1, f32[64,256]{1,0:T(8,128)} %bitcast.2, bf16[512,1024]{1,0:T(8,128)(2,1)} %outw_ref.1), custom_call_target="tpu_custom_call" | custom-call | tf_op jit(solution)/shard_map/pallas_call | solution.py:557
  31.6 0.7 %copy.9 = bf16[16,24,512]{2,1,0:T(8,128)(2,1)} copy(bf16[16,24,512]{2,1,0:T(8,128)(2,1)S(1)} %shard_map.73) | data formatting | bytes 786432

commit v4 on v3

--- a/solution.py
+++ b/solution.py
@@ -136,6 +136,8 @@
     rowh,
     colh,
     edge,
+    corners,
+    cornh,
     small,
     qkvw,
     wout,
@@ -214,7 +216,12 @@
     local[0].wait()
     last = pbuf[core, :, 16:24, :].astype(F32)[:, 7:8, :]
     first = pbuf[core, :, 0:8, :].astype(F32)[:, 0:1, :]
-    edge[...] = jnp.where(col == 0, last, first).reshape(rows, half).astype(BF16)
+    border = jnp.where(col == 0, last, first).reshape(rows, half)
+    edge[...] = border.astype(BF16)
+    for way, line in ((0, rows - 1), (1, 0)):
+        pieces = [border[line : line + 1, at : at + 128] for at in range(0, half, 128)]
+        blank = jnp.zeros((16 - len(pieces), 128), F32)
+        corners[way] = jnp.concatenate(pieces + [blank], axis=0).astype(BF16)
     pl.semaphore_wait(barrier, 2 * group - 1)
 
     above, below = tile > 0, tile < tiles - 1
@@ -232,8 +239,8 @@
 
     def col_copy(way, target):
         return remote(
-            edge,
-            colh.at[core, way],
+            edge if way == 0 else corners.at[way - 1],
+            colh.at[core] if way == 0 else cornh.at[core, way - 1],
             col_ssem.at[way, target],
             col_rsem.at[core, way],
             tile=tile + (0, 1, -1)[way],
@@ -299,9 +306,9 @@
         slot = core if target == 0 else other
         lanes = pl.ds(pl.multiple_of(slot * half, half), half)
         remote(
-            edge, colh.at[slot, 0], col_ssem.at[0, 0], col_rsem.at[slot, 0], mp=other
+            edge, colh.at[slot], col_ssem.at[0, 0], col_rsem.at[slot, 0], mp=other
         ).wait_recv()
-        beside = colh[slot, 0].astype(F32)
+        beside = colh[slot].astype(F32)
         zero = jnp.zeros_like(beside)
         left = jnp.where(col == 1, beside, zero)
         right = jnp.where(col == 0, beside, zero)
@@ -320,15 +327,17 @@
                     mp=other,
                 ).wait_recv()
                 remote(
-                    edge,
-                    colh.at[slot, way + 1],
+                    corners.at[0],
+                    cornh.at[slot, way],
                     col_ssem.at[0, 0],
                     col_rsem.at[slot, way + 1],
                     mp=other,
                 ).wait_recv()
                 padded[line, 8 : 8 + cols, lanes] = rowh[slot, way].astype(F32)
-                at = rows - 1 if way == 0 else 0
-                corner = colh[slot, way + 1].astype(F32)[at : at + 1, :]
+                packed = cornh[slot, way].astype(F32)
+                corner = jnp.concatenate(
+                    [packed[k : k + 1, :] for k in range(half // 128)], axis=1
+                )
                 blank = jnp.zeros_like(corner)
                 padded[line, 7:8, lanes] = jnp.where(col == 1, corner, blank)
                 padded[line, 8 + cols : 9 + cols, lanes] = jnp.where(col == 0, corner, blank)
@@ -567,8 +576,10 @@
             vmem((2, rows, cols, half), BF16),
             vmem((rows + 2, cols + 16, 2 * half), F32),
             vmem((2, 2, cols, half), BF16),
-            vmem((2, 3, rows, half), BF16),
+            vmem((2, rows, half), BF16),
             vmem((rows, half), BF16),
+            vmem((2, 16, 128), BF16),
+            vmem((2, 2, 16, 128), BF16),
             vmem((2, 16, half), F32),
             vmem(qkv_weight.shape, BF16),
             vmem((2, half, half), BF16),

time: 32.5 us -> 31.9 us (0.982)
  Pallas kernels: 31.6 us -> 31 us
    pallas_call x1, Pallas kernels: 31.6 us -> 31 us  [fused(): pl.pallas_call(functools.partial(layer_kernel, tiles), out_shape=pltpu.VM...]
where the time goes in v4:
time: 31.9 us; the launch traced here: 31.7 us
  Pallas kernels  31 us (97%)
  local copies, waits for them, and re-layouts  0.75 us (2%)
    pallas_call x1, Pallas kernels, fused(): pl.pallas_call(functools.partial(layer_kernel, tiles), out_shape=pltpu.VM...  31 us
    unnamed x1, local copies, waits for them, and re-layouts  0.75 us

profile of v4, /device:TPU:29, one launch (start us, length us, event | category | flops | bytes accessed | tf_op | source)
XLA Modules:
  0.0 31.7 jit_solution(10309579433860317397)
XLA Ops:
  0.0 31.0 %shard_map.73 = bf16[16,24,512]{2,1,0:T(8,128)(2,1)S(1)} custom-call(bf16[16,24,512]{2,1,0:T(8,128)(2,1)} %patches_ref.1, s32[16,24]{1,0:T(8,128)} %tissue_hbm.1, bf16[3,3,512]{2,1,0:T(4,128)(2,1)} %conv_hbm.1, f32[1,512]{1,0:T(1,128)} %bitcast.3, bf16[3,1024,512]{2,1,0:T(8,128)(2,1)} %qkv_ref.1, f32[64,256]{1,0:T(8,128)} %bitcast.2, bf16[512,1024]{1,0:T(8,128)(2,1)} %outw_ref.1), custom_call_target="tpu_custom_call" | custom-call | tf_op jit(solution)/shard_map/pallas_call | solution.py:566
  31.0 0.7 %copy.9 = bf16[16,24,512]{2,1,0:T(8,128)(2,1)} copy(bf16[16,24,512]{2,1,0:T(8,128)(2,1)S(1)} %shard_map.73) | data formatting | bytes 786432
